TPU v7x, 512 devices: a whole 4x4x16 slice. The times are simulated.
512 devices in a mesh: facet: 16 (over y, x_lo, core), sub: 32 (over x_hi, z).
Axes of the slice: x: 4 (x_hi: 2, x_lo: 2; x = x_hi * 2 + x_lo), y: 4, z: 16, core: 2. Of those that a mesh axis runs over, the one named last changes fastest.
Arguments:
- facet_image: bfloat16 [16, 32, 64, 16384], P('facet', 'sub'), may hold values from -6 to 6
- correction: float32 [16, 16384], P('facet'), may hold values from 0.5 to 2
- facet_sizes: int32 [16], P('facet'), may hold values from 8192 to 16384, as said below
- facet_offsets: int32 [16], P('facet'), may hold values from 0 to 262143
- counts: int32 [16], P('facet'), may hold values from 8 to 32, as said below
- sub_lists: int32 [16, 32], P('facet'), may hold values from 0 to 31, each once within a row
- sub_offsets: int32 [32], replicated, may hold values from 0 to 16383
- window: float32 [512], replicated, may hold values from 0.5 to 2
Outputs:
- subgrids: float32 [32, 2, 32, 64, 512], P('sub', None, None, 'facet')
Inputs may be any that keep to these rules, and one draw needn't show every extreme that they name: `facet_sizes`: every facet has at least half of 16384 rows, and some facet has exactly 16384. Some facet contributes to all 32 subgrids; only the first counts[f] slots of a facet's list are used. `sub_lists`: each facet's list names every subgrid once.
All inputs are finite; a program needn't handle non-finite values.
Results may differ from a plain program's by a relative error of at most 0.015.
Values may be sent and summed in bfloat16 or wider, within the bound.
A program may use at most 64 MiB of HBM per device.

v0:
```python
import math

import jax
import jax.numpy as jnp
from jax import lax
from jax.sharding import PartitionSpec as P

P_SIZE = 16384
SPLIT = 128
XM = 512
KD = 64


per_group = 8


def cos_sin(count_left, count_right, period, factor):
    left_ids = jnp.arange(count_left, dtype=jnp.int32)[:, None]
    right_ids = jnp.arange(count_right, dtype=jnp.int32)[None, :]
    phase_angle = (left_ids * right_ids % period).astype(jnp.float32) * (2.0 * math.pi / period)
    return (jnp.cos(phase_angle) * factor, jnp.sin(phase_angle) * factor)


def make_tables():
    cos_one, sin_one = cos_sin(SPLIT, SPLIT, SPLIT, 1.0 / math.sqrt(SPLIT))
    table_one = jnp.concatenate([cos_one, -sin_one], axis=0).astype(jnp.bfloat16)
    turn_cos, turn_sin = cos_sin(SPLIT, P_SIZE // SPLIT, P_SIZE, 1.0)
    span_len = P_SIZE // SPLIT
    cos_two, sin_two = cos_sin(span_len, span_len, span_len, 1.0 / math.sqrt(span_len))
    upper_two = jnp.concatenate([cos_two, -sin_two], axis=1)
    lower_two = jnp.concatenate([sin_two, cos_two], axis=1)
    table_two = jnp.concatenate([upper_two, lower_two], axis=0).astype(jnp.bfloat16)
    cos_three, sin_three = cos_sin(XM, XM, XM, 1.0 / math.sqrt(XM))
    upper_three = jnp.stack([cos_three, sin_three], axis=1)
    lower_three = jnp.stack([-sin_three, cos_three], axis=1)
    table_three = jnp.concatenate([upper_three, lower_three], axis=0).astype(jnp.bfloat16)
    return (table_one, turn_cos, turn_sin, table_two, table_three)


def prepare(columns, gains, limit, tables):
    table_one, turn_cos, turn_sin, table_two, table_three = tables
    column_count = columns.shape[0]
    span_len = P_SIZE // SPLIT
    positions = jnp.arange(P_SIZE, dtype=jnp.int32)
    masked = jnp.where(
        positions[None, :] < limit, columns.astype(jnp.float32) * gains[None, :], 0.0
    ).astype(jnp.bfloat16)
    split_rows = masked.reshape(column_count, SPLIT, span_len)
    section_one = jnp.einsum(
        "ra,kab->krb", table_one, split_rows, preferred_element_type=jnp.float32
    )
    real_part = section_one[:, :SPLIT]
    imag_part = section_one[:, SPLIT:]
    turned = jnp.concatenate(
        [real_part * turn_cos + imag_part * turn_sin, imag_part * turn_cos - real_part * turn_sin],
        axis=2,
    ).astype(jnp.bfloat16)
    spectrum = jnp.einsum(
        "kut,tw->kuw", turned, table_two, preferred_element_type=jnp.float32
    ).astype(jnp.bfloat16)
    return (
        spectrum.reshape(column_count, SPLIT, 2, span_len)
        .transpose(0, 2, 3, 1)
        .reshape(column_count, 2, P_SIZE)
    )


def extract(prepared, shifts, offset, window, table_three):
    extended = jnp.concatenate([prepared, prepared[:, :, :XM]], axis=2)
    pieces = jax.vmap(lambda shift_one: lax.dynamic_slice_in_dim(extended, shift_one, XM, axis=2))(
        shifts
    )
    freqs = (shifts[:, None] + jnp.arange(XM, dtype=jnp.int32)[None, :]) % P_SIZE
    turns = freqs * (offset % P_SIZE) % P_SIZE
    phase_angle = turns.astype(jnp.float32) * (2.0 * math.pi / P_SIZE)
    cosine = jnp.cos(phase_angle)[:, None, :]
    sine = jnp.sin(phase_angle)[:, None, :]
    real_part = pieces[:, :, 0].astype(jnp.float32)
    imag_part = pieces[:, :, 1].astype(jnp.float32)
    spectrum = jnp.concatenate(
        [
            window * (real_part * cosine + imag_part * sine),
            window * (imag_part * cosine - real_part * sine),
        ],
        axis=2,
    ).astype(jnp.bfloat16)
    result = jnp.einsum("lkt,thm->lhkm", spectrum, table_three, preferred_element_type=jnp.float32)
    return result.astype(jnp.bfloat16)


def local(
    facet_image, correction, facet_sizes, facet_offsets, counts, sub_lists, sub_offsets, window
):
    tables = make_tables()
    subgrid_total = sub_offsets.shape[0]
    prepared = prepare(facet_image[0, 0], correction[0], facet_sizes[0], tables)
    own_list = sub_lists[0]
    live_count = counts[0]
    own_offset = facet_offsets[0]
    subgrid_ids = jnp.arange(subgrid_total, dtype=jnp.int32)
    group_count = (live_count + per_group - 1) // per_group

    def add_group(number, dense_sum):
        first_slot = number * per_group
        chosen = lax.dynamic_slice_in_dim(own_list, first_slot, per_group)
        matches = chosen[:, None] == subgrid_ids[None, :]
        shifts = jnp.sum(jnp.where(matches, sub_offsets[None, :], 0), axis=1)
        contribution = extract(prepared, shifts, own_offset, window, tables[4])
        live = first_slot + jnp.arange(per_group, dtype=jnp.int32) < live_count
        selector = (matches & live[:, None]).astype(jnp.bfloat16)
        placed = jnp.einsum(
            "lg,lhkm->ghkm", selector, contribution, preferred_element_type=jnp.float32
        )
        return dense_sum + placed.astype(jnp.bfloat16)

    dense_sum = lax.fori_loop(
        0, group_count, add_group, jnp.zeros((subgrid_total, 2, KD, XM), jnp.bfloat16)
    )
    dense_sum = dense_sum[:, :, None]
    moved = lax.all_to_all(dense_sum, "sub", split_axis=0, concat_axis=2, tiled=True)
    return lax.psum_scatter(
        moved.astype(jnp.float32).astype(jnp.bfloat16), "facet", scatter_dimension=3, tiled=True
    ).astype(jnp.float32)


def solution(mesh):
    in_specs = (
        P("facet", "sub", None, None),
        P("facet", None),
        P("facet"),
        P("facet"),
        P("facet"),
        P("facet", None),
        P(),
        P(),
    )
    out_specs = P("sub", None, None, "facet", None)
    return jax.shard_map(local, mesh=mesh, in_specs=in_specs, out_specs=out_specs, check_vma=False)
```

profile of v0, /device:TPU:32, one launch (start us, length us, event | category | flops | bytes accessed | tf_op | source)
XLA Modules:
  0.0 478.3 jit_solution(3136776197779271419)
XLA Ops:
  7.9 0.3 negate_convert_fusion.1
  8.1 0.3 fusion.82
  8.4 0.3 fusion.81
  8.7 0.3 fusion.80
  8.9 4.4 negate_convert_fusion
  13.3 4.0 fusion.60
  17.4 1.9 convert_bitcast_fusion
  19.2 2.7 copy.46
  21.9 5.7 %copy.33 = f32[64,128,128]{1,2,0:T(8,128)} copy(f32[64,128,128]{2,1,0:T(8,128)} %bitcast.88) | data formatting | bytes 8388608 | tf_op jit(solution)/shard_map/convert_element_type | solution.py:46
  28.7 3.4 convolution_bitcast_fusion
  32.1 1.2 add_convert_fusion
  33.3 3.3 fusion.48
  36.6 6.9 %reshape.218 = bf16[64,128,2,128]{3,2,1,0:T(2,128)(2,1)} reshape(bf16[64,128,256]{2,1,0:T(8,128)(2,1)} %fusion.48) | data formatting | bytes 8388608 | tf_op jit(solution)/shard_map/reshape | solution.py:62
  43.5 21.8 %copy.37 = bf16[64,2,128,128]{0,1,3,2:T(2,128)(2,1)} copy(bf16[64,2,128,128]{2,1,3,0:T(2,128)(2,1)} %bitcast.87) | data formatting | bytes 8388608 | tf_op jit(solution)/shard_map/transpose | solution.py:63
  65.3 1.1 slice.35
  66.4 54.1 %pad_maximum_fusion = bf16[64,2,16896]{0,1,2:T(2,128)(2,1)} fusion(bf16[64,2,512]{0,1,2:T(2,128)(2,1)S(1)} %slice.35, bf16[64,2,16384]{0,1,2:T(2,128)(2,1)} %bitcast.86), kind=kLoop, calls=%fused_computation.49 | loop fusion | flops 2162688 | bytes 8650752 | tf_op jit(solution)/shard_map/while/body/concatenate | solution.py:69
  120.6 1.5 maximum_maximum_fusion
  122.0 2.5 broadcast_in_dim.34
  124.6 29.8 %while.13 = (s32[]{:T(128)}, bf16[32,2,64,512]{3,0,2,1:T(8,128)(2,1)}, s32[]{:T(128)}, s32[32]{0:T(128)S(1)}, s32[]{:T(128)}, /*index=5*/f32[512]{0:T(512)S(1)},...) while((s32[]{:T(128)}, ...), condition=%wide.region_2.3_spmd.clone, body=%wide.region_0.2_spmd.clone.sunk | while | flops 1123656960 | bytes 28379856 | solution.py:116
  124.8 0.2 fusion.96
  125.0 8.5 %gather_fusion = bf16[8,64,2,512]{1,2,3,0:T(2,128)(2,1)S(1)} fusion(bf16[64,2,16896]{0,1,2:T(2,128)(2,1)} %get-tuple-element.320, s32[8]{0:T(128)S(1)} %fusion.97), kind=kCustom, calls=%fused_computation.clone.clone.1 | custom fusion | bytes 2097248 | tf_op jit(solution)/shard_map/while/body/vmap()/gather | solution.py:70
  133.6 4.2 fusion.98
  137.8 3.0 copy.51
  140.8 3.9 copy.52
  144.8 2.2 fusion.100
  147.1 0.7 add_compare_fusion.3
  147.7 6.7 %convert_add_fusion.2 = bf16[32,2,64,512]{3,0,2,1:T(8,128)(2,1)} fusion(bf16[32,2,64,512]{3,0,2,1:T(8,128)(2,1)} %get-tuple-element.300, bf16[1024,2,512]{2,0,1:T(8,128)(2,1)S(1)} %copy-done, bf16[8,64,512]{2,0,1:T(8,128)(2,1)} %get-tuple-element.283, bf16[8,64,512]{2,0,1:T(8,128)(2,1)S(1)} %get-tuple-element.284, s32[8]{0:T(128)S(1)} %dynamic_slice.8, ...), kind=kOutput, calls=%fused_computation.2.clone.1 | convolution fusion | flops 1120403968 | bytes 11534376 | tf_op jit(solution)/shard_map/while/body/lg,lhkm->ghkm/dot_general | solution.py:111
  154.4 4.5 copy.48
  158.9 121.2 %all_to_all.18 = bf16[32,2,1,64,512]{4,3,1,2,0:T(8,128)(2,1)S(1)} all-to-all(bf16[32,2,1,64,512]{4,3,1,2,0:T(8,128)(2,1)S(1)} %bitcast.89), channel_id=1, replica_groups=mesh['facet'=16,'sub'=32] {'sub'}, dimensions={0} | all-to-all | bytes 8388608 | tf_op jit(solution)/shard_map/all_to_all | solution.py:120
  280.1 4.3 copy.39
  284.5 185.0 %reduce-scatter.2.cloned.1.call-done = bf16[1,2,32,4,512]{4,2,1,0,3:T(8,128)(2,1)} async-done(((bf16[1,2,32,64,512]{4,2,1,0,3:T(8,128)(2,1)}), bf16[1,2,32,4,512]{4,2,1,0,3:T(8,128)(2,1)}) %reduce-scatter.2.cloned.1.call-update) | async-done | bytes 262160 | tf_op jit(solution)/shard_map/reduce_scatter | solution.py:121
  469.5 1.9 copy.40
  (20 shorter events, 0.7 us)
Async XLA Ops:
  6.5 462.9 %reduce-scatter.2.cloned.1.call-start = ((), (), s32[]{:S(2)}) async-start(), calls=%async_computation.2 | async-start | bytes 4456448 | tf_op jit(solution)/shard_map/reduce_scatter | solution.py:121
  21.9 5.7 %copy-start.1 = (f32[1,16384]{1,0:T(1,128)S(1)}, f32[1,16384]{1,0:T(1,128)}, u32[]{:S(2)}) copy-start(f32[1,16384]{1,0:T(1,128)} %param.11) | copy-start | bytes 196612
  120.5 4.0 copy-start.2
  120.5 4.0 copy-start.3
  120.5 4.0 copy-start.4
  137.8 9.9 %copy-start = (bf16[1024,2,512]{2,0,1:T(8,128)(2,1)S(1)}, bf16[1024,2,512]{2,0,1:T(8,128)(2,1)}, u32[]{:S(2)}) copy-start(bf16[1024,2,512]{2,0,1:T(8,128)(2,1)} %get-tuple-element.322) | copy-start | bytes 6291460 | tf_op jit(solution)/shard_map/while
Sparse Core Ops, SparseCore 0:
  284.6 184.8 reduce-scatter.1
where the time goes:
time: 480 us; the launch traced here: 478 us
  waiting for transfers between devices  185 us (39%)
  blocking collectives  121 us (25%)
  local copies, waits for them, and re-layouts  71.6 us (15%)
  other arithmetic  71.3 us (15%)
  between operations  15.5 us (3%)
  matrix products  13.4 us (3%)
    reduce_scatter x1, waiting for transfers between devices, local(): lax.psum_scatter(moved.astype(jnp.float32).astype(jnp.bfloat16), 'facet',...  185 us
    all_to_all x1, blocking collectives, local(): lax.all_to_all(dense_sum, 'sub', split_axis=0, concat_axis=2, tiled=True)  121 us
    concatenate x1, other arithmetic, extract(): extended = jnp.concatenate([prepared, prepared[:, :, :XM]], axis=2)  54.1 us
    transpose x1, local copies, waits for them, and re-layouts, prepare(): return spectrum.reshape(column_count, SPLIT, 2, span_len).transpose(0, 2,...  21.8 us
    another operation x6, other arithmetic  12.4 us
  transfers between devices with their start and end apart: 1, of which 1 were waited for; matrix products, arithmetic and copies ran while one was open for 0% of the time, Pallas kernels for 0%

commit v1 on v0

v1 whole, which is shorter than its diff:
```python
import functools
import math

import jax
import jax.numpy as jnp
import ml_dtypes
import numpy as np
from jax import lax
from jax.experimental import pallas as pl
from jax.experimental.pallas import tpu as pltpu
from jax.sharding import PartitionSpec as P

N = 16384
XM = 512
KD = 64
SUBS = 32
GROUPS = 2
PER = SUBS // GROUPS
CHUNKS = 2 * GROUPS
ROWS = PER * 16
F32 = jnp.float32
BF16 = jnp.bfloat16
MESH = pl.DeviceIdType.MESH


def table_one():
    turns = np.outer(np.arange(128), np.arange(128)) % 128 * (2.0 * np.pi / 128)
    table = np.concatenate([np.cos(turns), -np.sin(turns)], axis=0) / math.sqrt(128.0)
    return table.astype(np.float32).astype(ml_dtypes.bfloat16)


def table_three():
    turns = np.outer(np.arange(XM), np.arange(XM)) % XM * (2.0 * np.pi / XM)
    cosine, sine = np.cos(turns), np.sin(turns)
    table = np.block([[cosine, sine], [-sine, cosine]]) / math.sqrt(XM)
    return table.astype(np.float32).astype(ml_dtypes.bfloat16)


def cos_turn(index):
    index = index & (N - 1)
    quarter = (index + 2048) >> 12
    angle = (index - (quarter << 12)).astype(F32) * (2.0 * math.pi / N)
    square = angle * angle
    even = 1.0 + square * (-0.5 + square * (1 / 24 + square * (-1 / 720 + square * (1 / 40320))))
    odd = angle * (1.0 + square * (-1 / 6 + square * (1 / 120 + square * (-1 / 5040))))
    value = jnp.where((quarter & 1) == 1, odd, even)
    return jnp.where(((quarter + 1) & 2) == 2, -value, value)


def iota(shape, axis):
    return lax.broadcasted_iota(jnp.int32, shape, axis)


def add_to(target, *others):
    def body(i, carry):
        rows = pl.ds(pl.multiple_of(i * 64, 64), 64)
        total = target[rows, :].astype(F32)
        for other in others:
            total = total + other[rows, :].astype(F32)
        target[rows, :] = total.astype(BF16)
        return carry

    lax.fori_loop(0, ROWS // 64, body, 0)


def kernel(
    image_hbm, gain_ref, size_ref, offset_ref, count_ref, starts_ref, list_ref, window_ref, one_ref, three_hbm,
    out_ref,
    image, three, plane, two, turn_cos, turn_sin, live, spec, parts, core_in, up_in, down_in, up_two, down_two,
    side_in, landed, scaled,
    image_sem, three_sem, core_send, core_recv, y_send, y_recv, x_send, x_recv, sub_send, sub_recv,
):
    f, s = lax.axis_index("facet"), lax.axis_index("sub")
    core, side, y = f % 2, (f // 2) % 2, f // 4
    core_peer = f + 1 - 2 * core
    side_peer = f + 2 - 4 * side
    up = ((y + 1) % 4) * 4 + f % 4
    down = ((y + 3) % 4) * 4 + f % 4

    loads = [
        pltpu.make_async_copy(
            image_hbm.at[:, pl.ds(part * 4096, 4096)], image.at[:, pl.ds(part * 4096, 4096)], image_sem.at[part]
        )
        for part in range(4)
    ]
    for load in loads:
        load.start()
    load_three = pltpu.make_async_copy(three_hbm, three, three_sem)
    load_three.start()

    barrier = pltpu.get_barrier_semaphore()
    for peer in (core_peer, side_peer, up, down):
        pl.semaphore_signal(barrier, inc=1, device_id={"facet": peer}, device_id_type=MESH)
    for step in range(1, SUBS):
        pl.semaphore_signal(barrier, inc=1, device_id={"sub": (s + step) % SUBS}, device_id_type=MESH)

    offset = offset_ref[0] & (N - 1)
    row, lane = iota((256, 256), 0), iota((256, 256), 1)
    freq = (row >> 3) * 4 + (row & 3)
    turns = freq * ((lane & 127) + offset) * 128 + 4096 * (((row >> 2) & 1) - (lane >> 7))
    two[...] = (cos_turn(turns) * (1.0 / math.sqrt(128.0))).astype(BF16)
    turns = iota((128, 128), 0) * (iota((128, 128), 1) + offset)
    turn_cos[...] = cos_turn(turns)
    turn_sin[...] = cos_turn(turns - 4096)
    named = (list_ref[...] == iota((SUBS, SUBS), 0)) & (iota((SUBS, SUBS), 1) < count_ref[0])
    live[...] = jnp.broadcast_to(jnp.sum(jnp.where(named, 1.0, 0.0), axis=1, keepdims=True), (SUBS, 128))

    size = size_ref[0]

    def fill(a, carry):
        first = pl.multiple_of(a * 128, 128)
        gain = jnp.where(iota((1, 128), 1) + first < size, gain_ref[:, pl.ds(first, 128)], 0.0)
        plane[pl.ds(pl.multiple_of(a * KD, KD), KD), :] = image[:, pl.ds(first, 128)].astype(F32) * gain
        return carry

    for part in range(4):
        loads[part].wait()
        lax.fori_loop(part * 32, part * 32 + 32, fill, 0, unroll=2)

    def transform(half, four):
        first = 4 * four + 2 * half
        columns = [plane[pl.ds(first + j, 128, stride=KD), :] for j in range(2)]
        section = jnp.dot(
            one_ref[...], jnp.concatenate(columns, axis=1).astype(BF16), preferred_element_type=F32
        )
        turned = []
        for j in range(2):
            re, im = section[:128, j * 128 : j * 128 + 128], section[128:, j * 128 : j * 128 + 128]
            cosine, sine = turn_cos[...], turn_sin[...]
            turned.append(
                jnp.concatenate([re * cosine + im * sine, im * cosine - re * sine], axis=1).astype(BF16)
            )
        result = lax.dot_general(
            two[...], jnp.concatenate(turned, axis=0), (((1,), (1,)), ((), ())), preferred_element_type=F32
        )
        for j in range(2):
            spec[half, four, j] = result[:, j * 128 : j * 128 + 128].reshape(32, 8, 128)

    def transforms(half, begin, end):
        def body(i, carry):
            transform(half, 2 * i)
            transform(half, 2 * i + 1)
            return carry

        lax.fori_loop(begin // 2, end // 2, body, 0)

    place = (iota((8, 128), 0) & 3) * 128 + iota((8, 128), 1)

    def extract(n):
        half, group = n // GROUPS, n % GROUPS

        def body(i, carry):
            g = i * GROUPS + group
            start = starts_ref[g]
            low = (start >> 9) & 31
            inside = place >= (start & 511)
            high = (low + 1) & 31
            weight = jnp.broadcast_to(live[pl.ds(g, 1), :], (8, 128))
            rows = pl.ds(pl.multiple_of(i * 16, 16), 16)
            for four in range(16):
                pair = [
                    jnp.where(inside, spec[half, four, j, low], spec[half, four, j, high]) * weight
                    for j in range(2)
                ]
                parts[n, four % 2, four // 4, (four // 2) % 2, rows, :] = jnp.concatenate(pair, axis=0).astype(BF16)
            return carry

        lax.fori_loop(0, PER, body, 0)

    def remote(source, target, send, recv, device):
        return pltpu.make_async_remote_copy(
            src_ref=source, dst_ref=target, send_sem=send, recv_sem=recv, device_id=device, device_id_type=MESH
        )

    started = []

    def go(copy):
        copy.start()
        started.append(copy)
        return copy

    opposite, above, below = (y + 2) % 4, (y + 1) % 4, (y + 3) % 4

    def core_start(n):
        return go(remote(parts.at[n, 1 - core], core_in.at[n], core_send.at[n], core_recv.at[n], {"facet": core_peer}))

    def first_start(n, core_copy):
        core_copy.wait_recv()
        mine = parts.at[n, core]

        def add(block, x):
            add_to(mine.at[block, x], core_in.at[n, block, x])

        def send(i, block, x, target, peer):
            return go(remote(mine.at[block, x], target, y_send.at[n, i], y_recv.at[n, i], {"facet": peer}))

        copies = [None] * 6
        add(opposite, 0)
        copies[0] = send(0, opposite, 0, up_in.at[n], up)
        add(opposite, 1)
        copies[1] = send(1, opposite, 1, down_in.at[n], down)
        add(above, 1)
        copies[2] = send(2, above, 1, up_two.at[n, 1], up)
        add(below, 0)
        copies[3] = send(3, below, 0, down_two.at[n, 0], down)
        add(above, 0)
        add(below, 1)
        add(y, 0)
        add(y, 1)
        return copies

    def second_start(n, copies):
        mine = parts.at[n, core]
        copies[0].wait_recv()
        add_to(mine.at[above, 0], up_in.at[n])
        copies[4] = go(
            remote(mine.at[above, 0], up_two.at[n, 0], y_send.at[n, 4], y_recv.at[n, 4], {"facet": up})
        )
        copies[1].wait_recv()
        add_to(mine.at[below, 1], down_in.at[n])
        copies[5] = go(
            remote(mine.at[below, 1], down_two.at[n, 1], y_send.at[n, 5], y_recv.at[n, 5], {"facet": down})
        )
        return copies

    def side_start(n, copies):
        mine = parts.at[n, core, y]
        for i in range(2, 6):
            copies[i].wait_recv()
        add_to(mine.at[1 - side], up_two.at[n, 1 - side], down_two.at[n, 1 - side])
        copy = go(remote(mine.at[1 - side], side_in.at[n], x_send.at[n], x_recv.at[n], {"facet": side_peer}))
        add_to(mine.at[side], up_two.at[n, side], down_two.at[n, side])
        return copy

    def sub_start(n, side_copy):
        half, group = n // GROUPS, n % GROUPS
        mine = parts.at[n, core, y, side]
        side_copy.wait_recv()
        add_to(mine, side_in.at[n])
        home = s // GROUPS
        for step in sorted(range(PER), key=lambda d: -min(d, PER - d)):
            i = (home + step) % PER
            block = mine.at[pl.ds(pl.multiple_of(i * 16, 16), 16), :]
            copy = remote(
                block, landed.at[half, s], sub_send.at[n], sub_recv.at[half], {"sub": i * GROUPS + group}
            )
            if step:
                copy.start()
            else:
                own = s % GROUPS == group

                @pl.when(own)
                def _():
                    landed[half, s] = block[...]

                @pl.when(jnp.logical_not(own))
                def _():
                    copy.start()

    transforms(0, 0, 16)
    core_copies, y_copies, side_copies = {}, {}, {}
    for step in range(CHUNKS + 4):
        if 0 <= step - 4 < CHUNKS:
            sub_start(step - 4, side_copies[step - 4])
        if 0 <= step - 3 < CHUNKS:
            side_copies[step - 3] = side_start(step - 3, y_copies[step - 3])
        if 0 <= step - 2 < CHUNKS:
            second_start(step - 2, y_copies[step - 2])
        if 0 <= step - 1 < CHUNKS:
            y_copies[step - 1] = first_start(step - 1, core_copies[step - 1])
        if step < CHUNKS:
            extract(step)
            if step == 0:
                pl.semaphore_wait(barrier, SUBS + 3)
            core_copies[step] = core_start(step)
        if step < GROUPS:
            transforms(1, step * (16 // GROUPS), (step + 1) * (16 // GROUPS))

    start = starts_ref[s]
    within = start & 511
    shift, blocks = within & 127, within >> 7
    turned_window = window_ref[...]
    for bit in range(7):
        turned_window = jnp.where(
            ((shift >> bit) & 1) == 1, pltpu.roll(turned_window, 1 << bit, 1), turned_window
        )
    block_of, lane_of = iota((8, 128), 0), iota((8, 128), 1)
    taken = (block_of - blocks - jnp.where(lane_of < shift, 1, 0)) & 3
    weight = jnp.zeros((8, 128), F32)
    for b in range(4):
        weight = jnp.where(taken == b, jnp.broadcast_to(turned_window[b : b + 1, :], (8, 128)), weight)
    weight = jnp.concatenate([weight, weight], axis=0)
    turns = ((iota((1, XM), 1) * within) & 511) * 32
    back_cos, back_sin = cos_turn(turns), cos_turn(turns - 4096)

    load_three.wait()
    for half in range(2):
        got = landed.at[half, pl.ds(0, SUBS - 1)]
        pltpu.make_async_copy(got, got, sub_recv.at[half]).wait()
    for half in range(2):
        for b in range(SUBS):
            scaled[pl.ds(b * 32 + half * 16, 16), :] = landed[half, b].astype(F32) * weight
    spectrum = jnp.concatenate(
        [scaled[pl.ds(i, 128, stride=8), :].astype(BF16) for i in range(8)], axis=1
    )
    result = jnp.dot(spectrum, three[...], preferred_element_type=F32)
    re, im = result[:, :XM], result[:, XM:]
    for h, value in enumerate((re * back_cos + im * back_sin, im * back_cos - re * back_sin)):
        for b in range(SUBS):
            out_ref[h, b] = value[4 * b : 4 * b + 4, :]

    for copy in started:
        copy.wait_send()
    for n in range(CHUNKS):
        own = s % GROUPS == n % GROUPS
        sent = parts.at[n, core, y, side]

        @pl.when(own)
        def _():
            some = sent.at[pl.ds(0, ROWS - 16), :]
            pltpu.make_async_copy(some, some, sub_send.at[n]).wait()

        @pl.when(jnp.logical_not(own))
        def _():
            pltpu.make_async_copy(sent, sent, sub_send.at[n]).wait()


def local(image, correction, sizes, offsets, counts, lists, starts, window):
    vmem, smem, anywhere = (pl.BlockSpec(memory_space=m) for m in (pltpu.VMEM, pltpu.SMEM, pl.ANY))
    block = (CHUNKS, ROWS, 128)
    out = pl.pallas_call(
        kernel,
        out_shape=jax.ShapeDtypeStruct((2, SUBS, 4, XM), F32),
        in_specs=[anywhere, vmem, smem, smem, smem, smem, vmem, vmem, vmem, anywhere],
        out_specs=vmem,
        scratch_shapes=[
            pltpu.VMEM((KD, N), BF16),
            pltpu.VMEM((1024, 1024), BF16),
            pltpu.VMEM((128 * KD, 128), F32),
            pltpu.VMEM((256, 256), BF16),
            pltpu.VMEM((128, 128), F32),
            pltpu.VMEM((128, 128), F32),
            pltpu.VMEM((SUBS, 128), F32),
            pltpu.VMEM((2, 16, 2, 32, 8, 128), F32),
            pltpu.VMEM((CHUNKS, 2, 4, 2, ROWS, 128), BF16),
            pltpu.VMEM((CHUNKS, 4, 2, ROWS, 128), BF16),
            pltpu.VMEM(block, BF16),
            pltpu.VMEM(block, BF16),
            pltpu.VMEM((CHUNKS, 2, ROWS, 128), BF16),
            pltpu.VMEM((CHUNKS, 2, ROWS, 128), BF16),
            pltpu.VMEM(block, BF16),
            pltpu.VMEM((2, SUBS, 16, 128), BF16),
            pltpu.VMEM((SUBS * 32, 128), F32),
            pltpu.SemaphoreType.DMA((4,)),
            pltpu.SemaphoreType.DMA,
            pltpu.SemaphoreType.DMA((CHUNKS,)),
            pltpu.SemaphoreType.DMA((CHUNKS,)),
            pltpu.SemaphoreType.DMA((CHUNKS, 6)),
            pltpu.SemaphoreType.DMA((CHUNKS, 6)),
            pltpu.SemaphoreType.DMA((CHUNKS,)),
            pltpu.SemaphoreType.DMA((CHUNKS,)),
            pltpu.SemaphoreType.DMA((CHUNKS,)),
            pltpu.SemaphoreType.DMA((2,)),
        ],
        compiler_params=pltpu.CompilerParams(
            collective_id=0, has_side_effects=True, vmem_limit_bytes=48 * 1024 * 1024
        ),
    )(
        image.reshape(KD, N), correction, sizes, offsets, counts, starts, lists, window.reshape(4, 128),
        jnp.asarray(table_one()), jnp.asarray(table_three()),
    )
    return out.reshape(1, 2, SUBS, 4, XM)


def solution(mesh):
    in_specs = (
        P("facet", "sub", None, None),
        P("facet", None),
        P("facet"),
        P("facet"),
        P("facet"),
        P("facet", None),
        P(),
        P(),
    )
    out_specs = P("sub", None, None, "facet", None)
    return jax.shard_map(local, mesh=mesh, in_specs=in_specs, out_specs=out_specs, check_vma=False)
```

time: 480 us -> 65.4 us (0.14)
  waiting for transfers between devices: 185 us -> 0 us
  blocking collectives: 121 us -> 0 us
  other arithmetic: 71.3 us -> 0 us
  local copies, waits for them, and re-layouts: 71.6 us -> 7.64 us
  Pallas kernels: 0 us -> 55.5 us
  between operations: 15.5 us -> 1.96 us
  matrix products: 13.4 us -> 0 us
    reduce_scatter x1 -> x0, waiting for transfers between devices: 185 us -> none  [local(): lax.psum_scatter(moved.astype(jnp.float32).astype(jnp.bfloat16), 'facet',...]
    all_to_all x1 -> x0, blocking collectives: 121 us -> none  [local(): lax.all_to_all(dense_sum, 'sub', split_axis=0, concat_axis=2, tiled=True)]
    concatenate x3 -> x0, other arithmetic: 55.6 us -> none  [the longest x1 54.1 us: extract(): extended = jnp.concatenate([prepared, prepared[:, :, :XM]], axis=2)]
    pallas_call x0 -> x1, Pallas kernels: none -> 55.5 us  [local(): pl.pallas_call(kernel, out_shape=jax.ShapeDtypeStruct((2, SUBS, 4, XM), F...]
    transpose x1 -> x0, local copies, waits for them, and re-layouts: 21.8 us -> none  [prepare(): return spectrum.reshape(column_count, SPLIT, 2, span_len).transpose(0, 2,...]
    dot_general x3 -> x0, matrix products: 13.4 us -> none  [the longest x1 6.68 us: add_group(): jnp.einsum('lg,lhkm->ghkm', selector, contribution, preferred_element_typ...]
    another operation x6 -> x0, other arithmetic: 12.4 us -> none
    while x5 -> x0, local copies, waits for them, and re-layouts: 11.4 us -> none
  transfers between devices with their start and end apart: 1 -> 0, of which waited for: 1 -> 0; matrix products, arithmetic and copies ran while one was open for 0% -> 0% of each run, Pallas kernels for 0% -> 0%
where the time goes in v1:
time: 65.4 us; the launch traced here: 65.1 us
  Pallas kernels  55.5 us (85%)
  local copies, waits for them, and re-layouts  7.64 us (12%)
  between operations  1.96 us (3%)
    pallas_call x1, Pallas kernels, local(): pl.pallas_call(kernel, out_shape=jax.ShapeDtypeStruct((2, SUBS, 4, XM), F...  55.5 us
    unnamed x15, local copies, waits for them, and re-layouts  7.64 us

profile of v1, /device:TPU:32, one launch (start us, length us, event | category | flops | bytes accessed | tf_op | source)
XLA Modules:
  0.0 65.1 jit_solution(3587501356771351409)
XLA Ops:
  1.9 0.0 copy-start
  2.0 1.6 %copy-done = bf16[1,1,64,16384]{3,2,1,0:T(8,128)(2,1)S(1)} copy-done((bf16[1,1,64,16384]{3,2,1,0:T(8,128)(2,1)S(1)}, bf16[1,1,64,16384]{3,2,1,0:T(8,128)(2,1)}, u32[]{:S(2)}) %copy-start) | copy-done | bytes 2097176
  3.5 0.0 copy-start.1
  3.5 1.6 %copy-done.1 = bf16[1024,1024]{1,0:T(8,128)(2,1)S(1)} copy-done((bf16[1024,1024]{1,0:T(8,128)(2,1)S(1)}, bf16[1024,1024]{1,0:T(8,128)(2,1)}, u32[]{:S(2)}) %copy-start.1) | copy-done | bytes 2097176
  5.1 0.0 copy-start.2
  5.1 0.8 %copy-done.2 = f32[1,16384]{1,0:T(1,128)S(1)} copy-done((f32[1,16384]{1,0:T(1,128)S(1)}, f32[1,16384]{1,0:T(1,128)}, u32[]{:S(2)}) %copy-start.2) | copy-done | bytes 65560
  6.0 0.0 copy-start.3
  6.0 0.8 %copy-done.3 = bf16[256,128]{1,0:T(8,128)(2,1)S(1)} copy-done((bf16[256,128]{1,0:T(8,128)(2,1)S(1)}, bf16[256,128]{1,0:T(8,128)(2,1)}, u32[]{:S(2)}) %copy-start.3) | copy-done | bytes 65560
  6.8 0.0 copy-start.4
  6.8 0.7 %copy-done.4 = f32[512]{0:T(512)S(1)} copy-done((f32[512]{0:T(512)S(1)}, f32[512]{0:T(512)}, u32[]{:S(2)}) %copy-start.4) | copy-done | bytes 2072
  7.5 0.0 copy-start.5
  7.5 0.7 %copy-done.5 = s32[32]{0:T(128)S(1)} copy-done((s32[32]{0:T(128)S(1)}, s32[32]{0:T(128)}, u32[]{:S(2)}) %copy-start.5) | copy-done | bytes 152
  8.1 0.0 copy-start.6
  8.1 0.7 %copy-done.6 = s32[1,32]{1,0:T(1,128)S(1)} copy-done((s32[1,32]{1,0:T(1,128)S(1)}, s32[1,32]{1,0:T(1,128)}, u32[]{:S(2)}) %copy-start.6) | copy-done | bytes 152
  8.8 55.5 %shard_map.100 = f32[2,32,4,512]{3,2,1,0:T(4,128)S(1)} custom-call(bf16[64,16384]{1,0:T(8,128)(2,1)S(1)} %bitcast.4, f32[1,16384]{1,0:T(1,128)S(1)} %copy-done.2, s32[1]{0:T(128)S(6)} %copy.12.size_ref, s32[1]{0:T(128)S(6)} %copy.13.offset_ref, s32[1]{0:T(128)S(6)} %copy.14.count_ref, s32[32]{0:T(128)S(1)} %copy-done.5, s32[1,32]{1,0:T(1,128)S(1)} %copy-done.6, ...), custom_call_target="tpu_custom_call" | custom-call | tf_op jit(solution)/shard_map/pallas_call | solution.py:331
  64.3 0.8 %copy.15 = f32[1,2,32,4,512]{4,3,2,1,0:T(4,128)} copy(f32[1,2,32,4,512]{4,3,2,1,0:T(4,128)S(1)} %bitcast.3) | data formatting | bytes 1048576
Async XLA Ops:
  1.9 1.6 %copy-start = (bf16[1,1,64,16384]{3,2,1,0:T(8,128)(2,1)S(1)}, bf16[1,1,64,16384]{3,2,1,0:T(8,128)(2,1)}, u32[]{:S(2)}) copy-start(bf16[1,1,64,16384]{3,2,1,0:T(8,128)(2,1)} %param.10) | copy-start | bytes 6291460
  3.5 1.6 %copy-start.1 = (bf16[1024,1024]{1,0:T(8,128)(2,1)S(1)}, bf16[1024,1024]{1,0:T(8,128)(2,1)}, u32[]{:S(2)}) copy-start(bf16[1024,1024]{1,0:T(8,128)(2,1)} %constant.5.clone.three_hbm) | copy-start | bytes 6291460
  5.1 0.8 %copy-start.2 = (f32[1,16384]{1,0:T(1,128)S(1)}, f32[1,16384]{1,0:T(1,128)}, u32[]{:S(2)}) copy-start(f32[1,16384]{1,0:T(1,128)} %gain_ref.1) | copy-start | bytes 196612
  6.0 0.8 %copy-start.3 = (bf16[256,128]{1,0:T(8,128)(2,1)S(1)}, bf16[256,128]{1,0:T(8,128)(2,1)}, u32[]{:S(2)}) copy-start(bf16[256,128]{1,0:T(8,128)(2,1)} %constant.4.clone.one_ref) | copy-start | bytes 196612
  6.8 0.7 %copy-start.4 = (f32[512]{0:T(512)S(1)}, f32[512]{0:T(512)}, u32[]{:S(2)}) copy-start(f32[512]{0:T(512)} %param.17) | copy-start | bytes 6148
  7.5 0.7 %copy-start.5 = (s32[32]{0:T(128)S(1)}, s32[32]{0:T(128)}, u32[]{:S(2)}) copy-start(s32[32]{0:T(128)} %starts_ref.1) | copy-start | bytes 388
  8.1 0.7 %copy-start.6 = (s32[1,32]{1,0:T(1,128)S(1)}, s32[1,32]{1,0:T(1,128)}, u32[]{:S(2)}) copy-start(s32[1,32]{1,0:T(1,128)} %list_ref.1) | copy-start | bytes 388

commit v2 on v1

v2 whole, which is shorter than its diff:
```python
import functools
import math

import jax
import jax.numpy as jnp
import ml_dtypes
import numpy as np
from jax import lax
from jax.experimental import pallas as pl
from jax.experimental.pallas import tpu as pltpu
from jax.sharding import PartitionSpec as P

N = 16384
XM = 512
KD = 64
SUBS = 32
GROUPS = 8
PER = SUBS // GROUPS
ROWS = PER * 32
HALF = ROWS // 2
ACROSS = (True, False, False, True, False, False, True, False)
ORDER = (
    ("T", 0), ("E", 0, 4), ("E", 0, 0), ("E", 0, 1), ("E", 0, 7), ("E", 0, 3), ("E", 0, 6), ("T", 1), ("E", 1, 6),
    ("E", 1, 2), ("E", 0, 2), ("S", 0, 0), ("E", 1, 0), ("E", 1, 3), ("E", 1, 1), ("A", 1), ("E", 0, 5), ("S", 0, 3),
    ("T", 2), ("E", 2, 1), ("B", 1), ("E", 2, 0), ("E", 2, 3), ("E", 2, 2), ("A", 2), ("B", 2), ("S", 1, 0),
    ("A", 0), ("T", 3), ("S", 1, 3), ("E", 3, 1), ("E", 3, 0), ("S", 2, 0), ("B", 0), ("E", 3, 4), ("E", 3, 5),
    ("E", 1, 4), ("O", 1), ("A", 4), ("A", 3), ("S", 2, 3), ("E", 3, 3), ("E", 2, 6), ("B", 3), ("E", 3, 7),
    ("E", 2, 4), ("B", 4), ("E", 1, 5), ("A", 5), ("E", 3, 6), ("E", 3, 2), ("E", 2, 5), ("B", 5), ("S", 3, 0),
    ("S", 0, 6), ("E", 2, 7), ("B", 7), ("L", 1), ("S", 1, 6), ("E", 1, 7), ("A", 7), ("O", 2), ("S", 3, 3),
    ("O", 0), ("S", 2, 6), ("O", 3), ("O", 4), ("S", 3, 6), ("L", 2), ("O", 5), ("A", 6), ("B", 6), ("L", 4),
    ("O", 7), ("L", 5), ("O", 6), ("L", 7),
)
F32 = jnp.float32
BF16 = jnp.bfloat16
MESH = pl.DeviceIdType.MESH


def table_one():
    turns = np.outer(np.arange(128), np.arange(128)) % 128 * (2.0 * np.pi / 128)
    table = np.concatenate([np.cos(turns), -np.sin(turns)], axis=0) / math.sqrt(128.0)
    return table.astype(np.float32).astype(ml_dtypes.bfloat16)


def table_three():
    turns = np.outer(np.arange(XM), np.arange(XM)) % XM * (2.0 * np.pi / XM)
    table = np.concatenate([np.cos(turns), np.sin(turns)], axis=1) / math.sqrt(XM)
    return table.astype(np.float32).astype(ml_dtypes.bfloat16)


def cos_turn(index):
    index = index & (N - 1)
    quarter = (index + 2048) >> 12
    angle = (index - (quarter << 12)).astype(F32) * (2.0 * math.pi / N)
    square = angle * angle
    even = 1.0 + square * (-0.5 + square * (1 / 24 + square * (-1 / 720 + square * (1 / 40320))))
    odd = angle * (1.0 + square * (-1 / 6 + square * (1 / 120 + square * (-1 / 5040))))
    value = jnp.where((quarter & 1) == 1, odd, even)
    return jnp.where(((quarter + 1) & 2) == 2, -value, value)


def iota(shape, axis):
    return lax.broadcasted_iota(jnp.int32, shape, axis)


def add_to(target, *others):
    count = target.shape[0]
    size = max(size for size in (16, 32, 48, 64, 80, 96, 128) if count % size == 0)

    def body(i, carry):
        rows = pl.ds(pl.multiple_of(i * size, size), size)
        total = target[rows, :].astype(F32)
        for other in others:
            total = total + other[rows, :].astype(F32)
        target[rows, :] = total.astype(BF16)
        return carry

    lax.fori_loop(0, count // size, body, 0)


def kernel(
    image_hbm, gain_hbm, size_hbm, offset_hbm, count_hbm, starts_hbm, list_hbm, window_hbm, one_hbm, three_hbm,
    out_ref,
    gain_ref, size_ref, offset_ref, count_ref, starts_ref, list_ref, window_ref, one_ref,
    image, three, plane, two, turn, live, given, taken, spec, parts, side_in, up_in, down_in, up_two, down_two,
    landed, scaled,
    small_sem, image_sem, three_sem, table_sem, given_sem, side_sem, y_sem, sub_send_sem, sub_recv_sem,
):
    f, s = lax.axis_index("facet"), lax.axis_index("sub")
    core, side, y = f % 2, (f // 2) % 2, f // 4
    core_peer = f + 1 - 2 * core
    side_peer = f + 2 - 4 * side
    up = ((y + 1) % 4) * 4 + f % 4
    down = ((y + 3) % 4) * 4 + f % 4

    small = [
        pltpu.make_async_copy(source, target, small_sem.at[i])
        for i, (source, target) in enumerate(
            (
                (offset_hbm, offset_ref), (count_hbm, count_ref), (list_hbm, list_ref), (size_hbm, size_ref), (gain_hbm, gain_ref), (one_hbm, one_ref),
                (starts_hbm, starts_ref), (window_hbm, window_ref),
            )
        )
    ]
    for load in small:
        load.start()
    loads = [
        pltpu.make_async_copy(
            image_hbm.at[:, pl.ds(part * 4096, 4096)], image.at[:, pl.ds(part * 4096, 4096)], image_sem.at[part]
        )
        for part in range(4)
    ]
    for load in loads:
        load.start()
    load_three = pltpu.make_async_copy(three_hbm, three, three_sem)
    load_three.start()

    barrier = pltpu.get_barrier_semaphore()
    for peer in (core_peer, side_peer, up, down):
        pl.semaphore_signal(barrier, inc=1, device_id={"facet": peer}, device_id_type=MESH)
    for step in range(1, SUBS):
        pl.semaphore_signal(barrier, inc=1, device_id={"sub": (s + step) % SUBS}, device_id_type=MESH)

    for load in small:
        load.wait()
    offset = offset_ref[0] & (N - 1)
    row, lane = iota((256, 256), 0), iota((256, 256), 1)
    freq = (row >> 3) * 4 + (row & 3)
    turns = freq * ((lane & 127) + offset) * 128 + 4096 * (((row >> 2) & 1) - (lane >> 7))
    two[0] = (cos_turn(turns) * (1.0 / math.sqrt(128.0))).astype(BF16)
    turns = iota((128, 128), 0) * (iota((128, 128), 1) + offset)
    turn[0, 0] = cos_turn(turns)
    turn[0, 1] = cos_turn(turns - 4096)
    named = (list_ref[...] == iota((SUBS, SUBS), 0)) & (iota((SUBS, SUBS), 1) < count_ref[0])
    live[0] = jnp.broadcast_to(jnp.sum(jnp.where(named, 1.0, 0.0), axis=1, keepdims=True), (SUBS, 128))

    started = []

    def go(source, target, send, recv, device):
        copy = pltpu.make_async_remote_copy(
            src_ref=source, dst_ref=target, send_sem=send, recv_sem=recv, device_id=device, device_id_type=MESH
        )
        copy.start()
        started.append(copy)
        return copy

    size = size_ref[0]

    def fill(a, carry):
        first = pl.multiple_of(a * 128, 128)
        gain = jnp.where(iota((1, 128), 1) + first < size, gain_ref[:, pl.ds(first, 128)], 0.0)
        plane[pl.ds(pl.multiple_of(a * KD, KD), KD), :] = image[:, pl.ds(first, 128)].astype(F32) * gain
        return carry

    for part in range(4):
        loads[part].wait()
        lax.fori_loop(part * 32, part * 32 + 32, fill, 0, unroll=2)

    block_y = ((y + 2) % 4, (y + 1) % 4, (y + 3) % 4, y)

    for q in range(4):
        for x in range(2):
            for j in range(4):
                column = 16 * block_y[q] + 8 * x + 4 * (1 - core) + j
                given[q, 4 * x + j] = plane[pl.ds(column, 128, stride=KD), :].astype(BF16)

    pl.semaphore_wait(barrier, SUBS + 3)
    tables = [
        go(table.at[0], table.at[1], table_sem.at[0, i], table_sem.at[1, i], {"facet": core_peer})
        for i, table in enumerate((two, turn, live))
    ]

    gifts = [
        go(given.at[q], taken.at[q], given_sem.at[0, q], given_sem.at[1, q], {"facet": core_peer}) for q in range(4)
    ]

    def transform(q, source, pair):
        if source == 0:
            first = 16 * block_y[q] + 8 * (pair // 2) + 4 * core + 2 * (pair % 2)
            columns = [plane[pl.ds(first + j, 128, stride=KD), :].astype(BF16) for j in range(2)]
        else:
            columns = [taken[q, 2 * pair + j] for j in range(2)]
        section = jnp.dot(one_ref[...], jnp.concatenate(columns, axis=1), preferred_element_type=F32)
        turned = []
        for j in range(2):
            re, im = section[:128, j * 128 : j * 128 + 128], section[128:, j * 128 : j * 128 + 128]
            cosine, sine = turn[source, 0], turn[source, 1]
            turned.append(
                jnp.concatenate([re * cosine + im * sine, im * cosine - re * sine], axis=1).astype(BF16)
            )
        result = lax.dot_general(
            two[source], jnp.concatenate(turned, axis=0), (((1,), (1,)), ((), ())), preferred_element_type=F32
        )
        for j in range(2):
            spec[q, source, pair, j] = result[:, j * 128 : j * 128 + 128].reshape(32, 8, 128)

    def transforms(q):
        if q > 0:
            gifts[q].wait_recv()
        for pair in range(4):
            transform(q, 0, pair)
        if q == 0:
            for table in tables:
                table.wait_recv()
            gifts[q].wait_recv()
        for pair in range(4):
            transform(q, 1, pair)

    place = (iota((8, 128), 0) & 3) * 128 + iota((8, 128), 1)

    def extract(q, m):
        def body(i, carry):
            g = i * GROUPS + m
            start = starts_ref[g]
            low = (start >> 9) & 31
            high = (low + 1) & 31
            inside = place >= (start & 511)
            weights = [jnp.broadcast_to(live[source, pl.ds(g, 1), :], (8, 128)) for source in range(2)]
            for pair in range(4):
                tiles = []
                for j in range(2):
                    windows = [
                        jnp.where(inside, spec[q, source, pair, j, low], spec[q, source, pair, j, high])
                        for source in range(2)
                    ]
                    tiles.append(windows[0] * weights[0] + windows[1] * weights[1])
                rows = pl.ds(pl.multiple_of(m * ROWS + i * 32 + (pair % 2) * 16, 16), 16)
                parts[q, pair // 2, rows, :] = jnp.concatenate(tiles, axis=0).astype(BF16)
            return carry

        lax.fori_loop(0, PER, body, 0, unroll=2)

    copies = {}

    def group(m):
        return pl.ds(m * ROWS, ROWS)

    def side_send(q, m):
        copies["side", q, m] = go(
            parts.at[q, 1 - side, group(m)], side_in.at[m, q],
            side_sem.at[0, q, m], side_sem.at[1, q, m], {"facet": side_peer},
        )

    def side_add(q, m):
        copies["side", q, m].wait_recv()
        add_to(parts.at[q, side, group(m)], side_in.at[m, q])

    def piece(q, m, p):
        if ACROSS[m]:
            return parts.at[q, side, pl.ds(m * ROWS + p * HALF, HALF)]
        return parts.at[q, p, group(m)]

    size_of = [pl.ds(0, HALF if across else ROWS) for across in ACROSS]

    def along_y(number, q, m, p, target, peer):
        copies["y", number, m] = go(
            piece(q, m, p), target, y_sem.at[0, number, m], y_sem.at[1, number, m], {"facet": peer}
        )

    def opposite_send(m):
        along_y(0, 0, m, 0, up_in.at[m, size_of[m]], up)
        along_y(1, 0, m, 1, down_in.at[m, size_of[m]], down)

    def above_send(m):
        along_y(2, 1, m, 1, up_two.at[m, 1, size_of[m]], up)

    def above_pass(m):
        copies["y", 0, m].wait_recv()
        add_to(piece(1, m, 0), up_in.at[m, size_of[m]])
        along_y(3, 1, m, 0, up_two.at[m, 0, size_of[m]], up)

    def below_send(m):
        along_y(4, 2, m, 0, down_two.at[m, 0, size_of[m]], down)

    def below_pass(m):
        copies["y", 1, m].wait_recv()
        add_to(piece(2, m, 1), down_in.at[m, size_of[m]])
        along_y(5, 2, m, 1, down_two.at[m, 1, size_of[m]], down)

    def own_add(m):
        for number in range(2, 6):
            copies["y", number, m].wait_recv()
        for p in range(2):
            add_to(piece(3, m, p), up_two.at[m, p, size_of[m]], down_two.at[m, p, size_of[m]])

    def sub_send(m):
        mine = parts.at[3, side]
        home = s // GROUPS
        for step in sorted(range(PER), key=lambda d: -min(d, PER - d)):
            i = (home + step) % PER
            block = mine.at[pl.ds(pl.multiple_of(m * ROWS + i * 32, 32), 32), :]
            copy = pltpu.make_async_remote_copy(
                src_ref=block, dst_ref=landed.at[s], send_sem=sub_send_sem.at[m], recv_sem=sub_recv_sem,
                device_id={"sub": i * GROUPS + m}, device_id_type=MESH,
            )
            if step:
                copy.start()
            else:
                own = s % GROUPS == m

                @pl.when(own)
                def _():
                    landed[s] = block[...]

                @pl.when(jnp.logical_not(own))
                def _():
                    copy.start()

    sends = (opposite_send, above_send, below_send, lambda m: None)

    def make(q, m):
        extract(q, m)
        if ACROSS[m]:
            side_send(q, m)
        else:
            sends[q](m)

    def side_take(q, m):
        side_add(q, m)
        sends[q](m)

    def own(m):
        own_add(m)
        if ACROSS[m]:
            sub_send(m)
        else:
            side_send(3, m)

    def last(m):
        side_add(3, m)
        sub_send(m)

    steps = {"T": transforms, "E": make, "S": side_take, "A": above_pass, "B": below_pass, "O": own, "L": last}
    for name, *place_of in ORDER:
        steps[name](*place_of)

    start = starts_ref[s]
    within = start & 511
    shift, blocks = within & 127, within >> 7
    turned_window = window_ref[...]
    for bit in range(7):
        turned_window = jnp.where(
            ((shift >> bit) & 1) == 1, pltpu.roll(turned_window, 1 << bit, 1), turned_window
        )
    block_of, lane_of = iota((8, 128), 0), iota((8, 128), 1)
    taken = (block_of - blocks - jnp.where(lane_of < shift, 1, 0)) & 3
    weight = jnp.zeros((8, 128), F32)
    for b in range(4):
        weight = jnp.where(taken == b, jnp.broadcast_to(turned_window[b : b + 1, :], (8, 128)), weight)
    weight = jnp.concatenate([weight] * 4, axis=0)
    turns = ((iota((1, XM), 1) * within) & 511) * 32
    back_cos, back_sin = cos_turn(turns), cos_turn(turns - 4096)

    load_three.wait()
    got = landed.at[pl.ds(0, SUBS - 1)]
    pltpu.make_async_copy(got, got, sub_recv_sem).wait()
    for b in range(SUBS):
        scaled[pl.ds(b * 32, 32), :] = landed[b].astype(F32) * weight
    spectrum = jnp.concatenate(
        [
            jnp.concatenate([scaled[pl.ds(4 * h + i, 128, stride=8), :].astype(BF16) for i in range(4)], axis=1)
            for h in range(2)
        ],
        axis=0,
    )
    result = jnp.dot(spectrum, three[...], preferred_element_type=F32)
    re = result[:128, :XM] - result[128:, XM:]
    im = result[:128, XM:] + result[128:, :XM]
    for h, value in enumerate((re * back_cos + im * back_sin, im * back_cos - re * back_sin)):
        for b in range(SUBS):
            out_ref[h, b] = value[4 * b : 4 * b + 4, :]

    for copy in started:
        copy.wait_send()
    for m in range(GROUPS):
        own = s % GROUPS == m
        sent = parts.at[3, side, group(m)]

        @pl.when(own)
        def _():
            some = sent.at[pl.ds(0, ROWS - 32), :]
            pltpu.make_async_copy(some, some, sub_send_sem.at[m]).wait()

        @pl.when(jnp.logical_not(own))
        def _():
            pltpu.make_async_copy(sent, sent, sub_send_sem.at[m]).wait()


def local(image, correction, sizes, offsets, counts, lists, starts, window):
    out = pl.pallas_call(
        kernel,
        out_shape=jax.ShapeDtypeStruct((2, SUBS, 4, XM), F32),
        in_specs=[pl.BlockSpec(memory_space=pltpu.HBM)] * 10,
        out_specs=pl.BlockSpec(memory_space=pltpu.VMEM),
        scratch_shapes=[
            pltpu.VMEM((1, N), F32),
            pltpu.SMEM((1,), jnp.int32),
            pltpu.SMEM((1,), jnp.int32),
            pltpu.SMEM((1,), jnp.int32),
            pltpu.SMEM((SUBS,), jnp.int32),
            pltpu.VMEM((1, SUBS), jnp.int32),
            pltpu.VMEM((4, 128), F32),
            pltpu.VMEM((256, 128), BF16),
            pltpu.VMEM((KD, N), BF16),
            pltpu.VMEM((XM, 2 * XM), BF16),
            pltpu.VMEM((128 * KD, 128), F32),
            pltpu.VMEM((2, 256, 256), BF16),
            pltpu.VMEM((2, 2, 128, 128), F32),
            pltpu.VMEM((2, SUBS, 128), F32),
            pltpu.VMEM((4, 8, 128, 128), BF16),
            pltpu.VMEM((4, 8, 128, 128), BF16),
            pltpu.VMEM((4, 2, 4, 2, 32, 8, 128), F32),
            pltpu.VMEM((4, 2, SUBS * 32, 128), BF16),
            pltpu.VMEM((GROUPS, 4, ROWS, 128), BF16),
            pltpu.VMEM((GROUPS, ROWS, 128), BF16),
            pltpu.VMEM((GROUPS, ROWS, 128), BF16),
            pltpu.VMEM((GROUPS, 2, ROWS, 128), BF16),
            pltpu.VMEM((GROUPS, 2, ROWS, 128), BF16),
            pltpu.VMEM((SUBS, 32, 128), BF16),
            pltpu.VMEM((SUBS * 32, 128), F32),
            pltpu.SemaphoreType.DMA((8,)),
            pltpu.SemaphoreType.DMA((4,)),
            pltpu.SemaphoreType.DMA,
            pltpu.SemaphoreType.DMA((2, 3)),
            pltpu.SemaphoreType.DMA((2, 4)),
            pltpu.SemaphoreType.DMA((2, 4, GROUPS)),
            pltpu.SemaphoreType.DMA((2, 6, GROUPS)),
            pltpu.SemaphoreType.DMA((GROUPS,)),
            pltpu.SemaphoreType.DMA,
        ],
        compiler_params=pltpu.CompilerParams(
            collective_id=0, has_side_effects=True, vmem_limit_bytes=64 * 1024 * 1024
        ),
    )(
        image.reshape(KD, N), correction, sizes, offsets, counts, starts, lists, window.reshape(4, 128),
        jnp.asarray(table_one()), jnp.asarray(table_three()),
    )
    return out.reshape(1, 2, SUBS, 4, XM)


def solution(mesh):
    in_specs = (
        P("facet", "sub", None, None),
        P("facet", None),
        P("facet"),
        P("facet"),
        P("facet"),
        P("facet", None),
        P(),
        P(),
    )
    out_specs = P("sub", None, None, "facet", None)
    return jax.shard_map(local, mesh=mesh, in_specs=in_specs, out_specs=out_specs, check_vma=False)
```

time: 65.4 us -> 52.4 us (0.80)
  the two profiles are of different devices: /device:TPU:32 before, /device:TPU:24 now
where the time goes in v2:
time: 52.4 us; the launch traced here: 52.3 us
  Pallas kernels  48.4 us (92%)
  between operations  1.95 us (4%)
  local copies, waits for them, and re-layouts  1.87 us (4%)
    pallas_call x1, Pallas kernels, local(): pl.pallas_call(kernel, out_shape=jax.ShapeDtypeStruct((2, SUBS, 4, XM), F...  48.4 us
    unnamed x1, local copies, waits for them, and re-layouts  1.87 us

profile of v2, /device:TPU:24, one launch (start us, length us, event | category | flops | bytes accessed | tf_op | source)
XLA Modules:
  0.0 52.3 jit_solution(13391781165106448540)
XLA Ops:
  1.9 48.4 %shard_map.100 = f32[2,32,4,512]{3,2,1,0:T(4,128)} custom-call(bf16[64,16384]{1,0:T(8,128)(2,1)} %bitcast.4, f32[1,16384]{1,0:T(1,128)} %gain_hbm.1, s32[1]{0:T(128)S(6)} %copy.12.size_hbm, s32[1]{0:T(128)S(6)} %copy.13.offset_hbm, s32[1]{0:T(128)S(6)} %copy.14.count_hbm, s32[32]{0:T(128)} %starts_hbm.1, s32[1,32]{1,0:T(1,128)} %list_hbm.1, ...), custom_call_target="tpu_custom_call" | custom-call | tf_op jit(solution)/shard_map/pallas_call | solution.py:389
  50.4 1.9 %copy.15 = f32[1,2,32,4,512]{4,3,2,1,0:T(4,128)} copy(f32[1,2,32,4,512]{4,3,2,1,0:T(4,128)} %bitcast.3) | data formatting | bytes 1048576

commit v3 on v2

--- a/solution.py
+++ b/solution.py
@@ -18,17 +18,17 @@
 PER = SUBS // GROUPS
 ROWS = PER * 32
 HALF = ROWS // 2
-ACROSS = (True, False, False, True, False, False, True, False)
+ACROSS = (True, False, True, False, True, False, False, False)
 ORDER = (
-    ("T", 0), ("E", 0, 4), ("E", 0, 0), ("E", 0, 1), ("E", 0, 7), ("E", 0, 3), ("E", 0, 6), ("T", 1), ("E", 1, 6),
-    ("E", 1, 2), ("E", 0, 2), ("S", 0, 0), ("E", 1, 0), ("E", 1, 3), ("E", 1, 1), ("A", 1), ("E", 0, 5), ("S", 0, 3),
-    ("T", 2), ("E", 2, 1), ("B", 1), ("E", 2, 0), ("E", 2, 3), ("E", 2, 2), ("A", 2), ("B", 2), ("S", 1, 0),
-    ("A", 0), ("T", 3), ("S", 1, 3), ("E", 3, 1), ("E", 3, 0), ("S", 2, 0), ("B", 0), ("E", 3, 4), ("E", 3, 5),
-    ("E", 1, 4), ("O", 1), ("A", 4), ("A", 3), ("S", 2, 3), ("E", 3, 3), ("E", 2, 6), ("B", 3), ("E", 3, 7),
-    ("E", 2, 4), ("B", 4), ("E", 1, 5), ("A", 5), ("E", 3, 6), ("E", 3, 2), ("E", 2, 5), ("B", 5), ("S", 3, 0),
-    ("S", 0, 6), ("E", 2, 7), ("B", 7), ("L", 1), ("S", 1, 6), ("E", 1, 7), ("A", 7), ("O", 2), ("S", 3, 3),
-    ("O", 0), ("S", 2, 6), ("O", 3), ("O", 4), ("S", 3, 6), ("L", 2), ("O", 5), ("A", 6), ("B", 6), ("L", 4),
-    ("O", 7), ("L", 5), ("O", 6), ("L", 7),
+    ("T", 0), ("E", 0, 3), ("E", 0, 0), ("E", 0, 4), ("E", 0, 7), ("E", 0, 2), ("E", 0, 6), ("E", 0, 5), ("E", 0, 1),
+    ("T", 1), ("E", 1, 4), ("E", 1, 3), ("S", 0, 0), ("E", 1, 2), ("A", 3), ("E", 1, 0), ("S", 0, 4), ("T", 2),
+    ("E", 2, 3), ("E", 2, 2), ("E", 2, 0), ("B", 3), ("E", 2, 1), ("E", 2, 4), ("S", 0, 2), ("B", 1), ("E", 1, 1),
+    ("A", 1), ("T", 3), ("E", 3, 3), ("E", 3, 2), ("S", 1, 0), ("S", 2, 2), ("E", 3, 1), ("A", 0), ("O", 3),
+    ("S", 2, 0), ("B", 0), ("E", 2, 5), ("B", 5), ("E", 3, 0), ("E", 1, 5), ("A", 5), ("B", 2), ("E", 3, 7),
+    ("E", 3, 4), ("S", 1, 2), ("A", 2), ("E", 2, 6), ("S", 3, 2), ("O", 1), ("B", 6), ("S", 1, 4), ("A", 4),
+    ("L", 3), ("E", 3, 5), ("E", 1, 6), ("A", 6), ("S", 2, 4), ("B", 4), ("E", 1, 7), ("S", 3, 0), ("O", 0),
+    ("A", 7), ("E", 2, 7), ("S", 3, 4), ("B", 7), ("E", 3, 6), ("O", 5), ("L", 1), ("O", 2), ("L", 5), ("O", 6),
+    ("O", 4), ("O", 7), ("L", 6), ("L", 7),
 )
 F32 = jnp.float32
 BF16 = jnp.bfloat16
@@ -91,6 +91,22 @@
     side_peer = f + 2 - 4 * side
     up = ((y + 1) % 4) * 4 + f % 4
     down = ((y + 3) % 4) * 4 + f % 4
+    high, z = s // 16, s % 16
+    taker = (side + high * (1 - 2 * side), side + (1 - high) * (1 - 2 * side))
+    target = (f + high * (2 - 4 * side), f + (1 - high) * (2 - 4 * side))
+
+    barrier = pltpu.get_barrier_semaphore()
+
+    def greet(device):
+        pl.semaphore_signal(barrier, inc=1, device_id=device, device_id_type=MESH)
+
+    for step in range(16):
+        there = (z + step) % 16
+        greet({"facet": side_peer, "sub": (1 - high) * 16 + there})
+        if step:
+            greet({"sub": high * 16 + there})
+    for peer in (core_peer, side_peer, up, down):
+        greet({"facet": peer})
 
     small = [
         pltpu.make_async_copy(source, target, small_sem.at[i])
@@ -113,12 +129,6 @@
         load.start()
     load_three = pltpu.make_async_copy(three_hbm, three, three_sem)
     load_three.start()
-
-    barrier = pltpu.get_barrier_semaphore()
-    for peer in (core_peer, side_peer, up, down):
-        pl.semaphore_signal(barrier, inc=1, device_id={"facet": peer}, device_id_type=MESH)
-    for step in range(1, SUBS):
-        pl.semaphore_signal(barrier, inc=1, device_id={"sub": (s + step) % SUBS}, device_id_type=MESH)
 
     for load in small:
         load.wait()
@@ -234,19 +244,24 @@
     def group(m):
         return pl.ds(m * ROWS, ROWS)
 
+    def half_of(m, h):
+        return pl.ds(m * ROWS + h * HALF, HALF)
+
     def side_send(q, m):
-        copies["side", q, m] = go(
-            parts.at[q, 1 - side, group(m)], side_in.at[m, q],
-            side_sem.at[0, q, m], side_sem.at[1, q, m], {"facet": side_peer},
-        )
+        for h in range(2):
+            copies["side", q, m, h] = go(
+                parts.at[q, 1 - taker[h], half_of(m, h)], side_in.at[m, q, pl.ds(h * HALF, HALF)],
+                side_sem.at[0, q, m, h], side_sem.at[1, q, m, h], {"facet": side_peer},
+            )
 
     def side_add(q, m):
-        copies["side", q, m].wait_recv()
-        add_to(parts.at[q, side, group(m)], side_in.at[m, q])
+        for h in range(2):
+            copies["side", q, m, h].wait_recv()
+            add_to(parts.at[q, taker[h], half_of(m, h)], side_in.at[m, q, pl.ds(h * HALF, HALF)])
 
     def piece(q, m, p):
         if ACROSS[m]:
-            return parts.at[q, side, pl.ds(m * ROWS + p * HALF, HALF)]
+            return parts.at[q, taker[p], half_of(m, p)]
         return parts.at[q, p, group(m)]
 
     size_of = [pl.ds(0, HALF if across else ROWS) for across in ACROSS]
@@ -283,27 +298,29 @@
             add_to(piece(3, m, p), up_two.at[m, p, size_of[m]], down_two.at[m, p, size_of[m]])
 
     def sub_send(m):
-        mine = parts.at[3, side]
-        home = s // GROUPS
-        for step in sorted(range(PER), key=lambda d: -min(d, PER - d)):
-            i = (home + step) % PER
-            block = mine.at[pl.ds(pl.multiple_of(m * ROWS + i * 32, 32), 32), :]
-            copy = pltpu.make_async_remote_copy(
-                src_ref=block, dst_ref=landed.at[s], send_sem=sub_send_sem.at[m], recv_sem=sub_recv_sem,
-                device_id={"sub": i * GROUPS + m}, device_id_type=MESH,
-            )
-            if step:
-                copy.start()
-            else:
-                own = s % GROUPS == m
-
-                @pl.when(own)
-                def _():
-                    landed[s] = block[...]
-
-                @pl.when(jnp.logical_not(own))
-                def _():
+        home = z // GROUPS
+        count = PER // 2
+        for step in sorted(range(count), key=lambda d: -min(d, count - d)):
+            i = (home + step) % count
+            for h in range(2):
+                row = m * ROWS + h * HALF + i * 32
+                block = parts.at[3, taker[h], pl.ds(pl.multiple_of(row, 32), 32), :]
+                copy = pltpu.make_async_remote_copy(
+                    src_ref=block, dst_ref=landed.at[s], send_sem=sub_send_sem.at[m], recv_sem=sub_recv_sem,
+                    device_id={"facet": target[h], "sub": h * 16 + i * GROUPS + m}, device_id_type=MESH,
+                )
+                if step:
                     copy.start()
+                else:
+                    own = jnp.logical_and(high == h, z % GROUPS == m)
+
+                    @pl.when(own)
+                    def _():
+                        landed[s] = block[...]
+
+                    @pl.when(jnp.logical_not(own))
+                    def _():
+                        copy.start()
 
     sends = (opposite_send, above_send, below_send, lambda m: None)
 
@@ -372,8 +389,8 @@
     for copy in started:
         copy.wait_send()
     for m in range(GROUPS):
-        own = s % GROUPS == m
-        sent = parts.at[3, side, group(m)]
+        own = z % GROUPS == m
+        sent = parts.at[3, 0, group(m)]
 
         @pl.when(own)
         def _():
@@ -422,7 +439,7 @@
             pltpu.SemaphoreType.DMA,
             pltpu.SemaphoreType.DMA((2, 3)),
             pltpu.SemaphoreType.DMA((2, 4)),
-            pltpu.SemaphoreType.DMA((2, 4, GROUPS)),
+            pltpu.SemaphoreType.DMA((2, 4, GROUPS, 2)),
             pltpu.SemaphoreType.DMA((2, 6, GROUPS)),
             pltpu.SemaphoreType.DMA((GROUPS,)),
             pltpu.SemaphoreType.DMA,

time: 52.4 us -> 51.7 us (0.987)
  the two profiles are of different devices: /device:TPU:24 before, /device:TPU:128 now
where the time goes in v3:
time: 51.7 us; the launch traced here: 51.5 us
  Pallas kernels  47.6 us (92%)
  between operations  1.95 us (4%)
  local copies, waits for them, and re-layouts  1.87 us (4%)
    pallas_call x1, Pallas kernels, local(): pl.pallas_call(kernel, out_shape=jax.ShapeDtypeStruct((2, SUBS, 4, XM), F...  47.6 us
    unnamed x1, local copies, waits for them, and re-layouts  1.87 us

profile of v3, /device:TPU:128, one launch (start us, length us, event | category | flops | bytes accessed | tf_op | source)
XLA Modules:
  0.0 51.5 jit_solution(11288645101670864886)
XLA Ops:
  1.9 47.6 %shard_map.100 = f32[2,32,4,512]{3,2,1,0:T(4,128)} custom-call(bf16[64,16384]{1,0:T(8,128)(2,1)} %bitcast.4, f32[1,16384]{1,0:T(1,128)} %gain_hbm.1, s32[1]{0:T(128)S(6)} %copy.12.size_hbm, s32[1]{0:T(128)S(6)} %copy.13.offset_hbm, s32[1]{0:T(128)S(6)} %copy.14.count_hbm, s32[32]{0:T(128)} %starts_hbm.1, s32[1,32]{1,0:T(1,128)} %list_hbm.1, ...), custom_call_target="tpu_custom_call" | custom-call | tf_op jit(solution)/shard_map/pallas_call | solution.py:406
  49.6 1.9 %copy.15 = f32[1,2,32,4,512]{4,3,2,1,0:T(4,128)} copy(f32[1,2,32,4,512]{4,3,2,1,0:T(4,128)} %bitcast.3) | data formatting | bytes 1048576

commit v4 on v3

--- a/solution.py
+++ b/solution.py
@@ -204,13 +204,15 @@
             spec[q, source, pair, j] = result[:, j * 128 : j * 128 + 128].reshape(32, 8, 128)
 
     def transforms(q):
-        if q > 0:
+        if q > 1:
             gifts[q].wait_recv()
-        for pair in range(4):
-            transform(q, 0, pair)
+        for block in ((0, 1), (), (2,), (3,))[q]:
+            for pair in range(4):
+                transform(block, 0, pair)
         if q == 0:
             for table in tables:
                 table.wait_recv()
+        if q < 2:
             gifts[q].wait_recv()
         for pair in range(4):
             transform(q, 1, pair)

time: 51.7 us -> 51.7 us (level)
  the two profiles are of different devices: /device:TPU:128 before, /device:TPU:16 now
where the time goes in v4:
time: 51.7 us; the launch traced here: 51.5 us
  Pallas kernels  47.7 us (92%)
  between operations  1.95 us (4%)
  local copies, waits for them, and re-layouts  1.87 us (4%)
    pallas_call x1, Pallas kernels, local(): pl.pallas_call(kernel, out_shape=jax.ShapeDtypeStruct((2, SUBS, 4, XM), F...  47.7 us
    unnamed x1, local copies, waits for them, and re-layouts  1.87 us

profile of v4, /device:TPU:16, one launch (start us, length us, event | category | flops | bytes accessed | tf_op | source)
XLA Modules:
  0.0 51.5 jit_solution(6686933250851978458)
XLA Ops:
  1.9 47.7 %shard_map.100 = f32[2,32,4,512]{3,2,1,0:T(4,128)} custom-call(bf16[64,16384]{1,0:T(8,128)(2,1)} %bitcast.4, f32[1,16384]{1,0:T(1,128)} %gain_hbm.1, s32[1]{0:T(128)S(6)} %copy.12.size_hbm, s32[1]{0:T(128)S(6)} %copy.13.offset_hbm, s32[1]{0:T(128)S(6)} %copy.14.count_hbm, s32[32]{0:T(128)} %starts_hbm.1, s32[1,32]{1,0:T(1,128)} %list_hbm.1, ...), custom_call_target="tpu_custom_call" | custom-call | tf_op jit(solution)/shard_map/pallas_call | solution.py:408
  49.6 1.9 %copy.15 = f32[1,2,32,4,512]{4,3,2,1,0:T(4,128)} copy(f32[1,2,32,4,512]{4,3,2,1,0:T(4,128)} %bitcast.3) | data formatting | bytes 1048576
